TPU v7x, 256 devices: a whole 4x4x8 slice. The times are simulated.
256 devices in a mesh: row: 16 (over z, core), col: 16 (over x, y).
Axes of the slice: x: 4, y: 4, z: 8, core: 2. Of those that a mesh axis runs over, the one named last changes fastest.
Arguments:
- out_grad: bfloat16 [65536, 128], P(('row', 'col')), may hold values from -6 to 6
- relu_mask: bfloat16 [65536, 128], P(('row', 'col')), may hold values from 0 to 1, as said below
- saved_agg: bfloat16 [65536, 128], P(('row', 'col')), may hold values from -0.059814453 to 0.059814453
- weight: bfloat16 [128, 128], replicated, may hold values from -0.5 to 0.5
- tile_values: bfloat16 [16, 16, 320, 128, 128], P('row', 'col'), may hold values from 0 to 0.012084961
- tile_coords: int32 [16, 16, 320, 2], P('row', 'col'), may hold values from 0 to 31, as said below
- tile_count: int32 [16, 16], P('row', 'col'), may hold values from 80 to 320, as said below
Outputs:
- input_grad: bfloat16 [65536, 128], P(('col', 'row'))
- weight_grad: float32 [128, 128], replicated
Inputs may be any that keep to these rules, and one draw needn't show every extreme that they name: `tile_coords`: within one block the live and dead slots name distinct tiles; tile rows are below 32, tile columns below 32. Slots at or past tile_count are ignored. `tile_count`: live slots of a block; some block is full in every draw. `relu_mask`: entries are 0 or 1.
All inputs are finite; a program needn't handle non-finite values.
Results may differ from a plain program's by a relative error of at most 0.0049.
Values may be sent and summed in bfloat16 or wider, within the bound.
A program may use at most 128 MiB of HBM per device.

v0:
```python
import jax
import jax.numpy as jnp
from jax import lax
from jax.sharding import PartitionSpec as P


def local(out_grad, relu_mask, saved_agg, weight, tile_values, tile_coords, tile_count):
    tile_size = tile_values.shape[-1]
    slot_count = tile_values.shape[2]
    feature_width = weight.shape[0]
    pre_grad = (out_grad.astype(jnp.float32) * relu_mask.astype(jnp.float32)).astype(jnp.bfloat16)
    term = lax.dot_general(
        saved_agg, pre_grad, (((0,), (0,)), ((), ())), preferred_element_type=jnp.float32
    )
    weight_grad = lax.psum(term, ("row", "col"))
    grad_rows = lax.all_gather(pre_grad, "col", axis=0, tiled=True)
    agg_rows = jnp.dot(grad_rows, weight.T, preferred_element_type=jnp.float32).astype(jnp.bfloat16)
    panel_tiles = agg_rows.reshape(-1, tile_size, feature_width)
    coords = tile_coords[0, 0]
    values = tile_values[0, 0]
    alive = (jnp.arange(slot_count, dtype=jnp.int32) < tile_count[0, 0]).astype(jnp.float32)
    gathered = panel_tiles[coords[:, 0]]
    products = jnp.einsum("kab,kaf->kbf", values, gathered, preferred_element_type=jnp.float32)
    live_products = products * alive[:, None, None]
    node_rows = out_grad.shape[0]
    column_tiles = node_rows * lax.axis_size("row") // tile_size
    column_ids = coords[:, 1]
    partial_value = jax.ops.segment_sum(live_products, column_ids, num_segments=column_tiles)
    partial_value = partial_value.reshape(column_tiles * tile_size, feature_width)
    summed = lax.psum_scatter(partial_value, "row", scatter_dimension=0, tiled=True)
    input_grad = summed.astype(jnp.bfloat16)
    return (input_grad, weight_grad)


def solution(mesh):
    in_specs = (
        P(("row", "col"), None),
        P(("row", "col"), None),
        P(("row", "col"), None),
        P(),
        P("row", "col", None, None, None),
        P("row", "col", None, None),
        P("row", "col"),
    )
    out_specs = (P(("col", "row"), None), P())
    return jax.shard_map(local, mesh=mesh, in_specs=in_specs, out_specs=out_specs, check_vma=False)
```

profile of v0, /device:TPU:1, one launch (start us, length us, event | category | flops | bytes accessed | tf_op | source)
XLA Modules:
  0.0 270.3 jit_solution(11169470744619488554)
XLA Ops:
  8.0 0.0 copy-start
  8.0 0.0 all-gather.2.cloned.1.call-start
  8.1 1.5 multiply_convert_fusion
  9.6 0.0 all-gather.2.cloned.1.call-update
  9.6 0.0 all-reduce.2.cloned.1.call-start
  9.7 0.0 copy-done
  9.7 1.7 convolution_bitcast_fusion
  11.3 0.0 all-reduce.2.cloned.1.call-update
  11.4 0.0 reduce-scatter.2.cloned.1.call-start
  11.4 0.8 fusion.5
  12.9 49.2 %all-gather.2.cloned.1.call-done = bf16[4096,128]{1,0:T(8,128)(2,1)} async-done(((bf16[256,128]{1,0:T(8,128)(2,1)}), bf16[4096,128]{1,0:T(8,128)(2,1)}) %all-gather.2.cloned.1.call-update) | async-done | bytes 1048592 | tf_op jit(solution)/shard_map/all_gather | solution.py:16
  62.1 1.7 convolution_convert_fusion
  63.7 10.7 %gather_fusion = bf16[320,128,128]{2,1,0:T(8,128)(2,1)} fusion(bf16[32,128,128]{2,1,0:T(8,128)(2,1)S(1)} %bitcast.20, s32[1024]{0:T(1024)S(1)} %pad_clamp_fusion), kind=kCustom, calls=%fused_computation | custom fusion | bytes 20972800 | tf_op jit(solution)/shard_map/gather | solution.py:22
  74.5 13.6 %multiply_bitcast_fusion = f32[320,128,128]{1,2,0:T(8,128)} fusion(f32[320]{0:T(512)S(1)} %fusion.4, bf16[320,128,128]{2,1,0:T(8,128)(2,1)} %gather_fusion, bf16[1,1,320,128,128]{4,3,2,1,0:T(8,128)(2,1)} %param.11), kind=kOutput, calls=%fused_computation.2 | convolution fusion | flops 1347420160 | bytes 41944320 | tf_op jit(solution)/shard_map/kab,kaf->kbf/dot_general | solution.py:23
  88.1 21.1 %copy.12 = f32[320,128,128]{2,1,0:T(8,128)} copy(f32[320,128,128]{1,2,0:T(8,128)} %multiply_bitcast_fusion) | data formatting | bytes 41943040 | tf_op jit(solution)/shard_map/mul | solution.py:24
  109.2 0.2 broadcast_in_dim.2
  109.4 0.0 copy-start.1
  109.4 42.0 %scatter_fusion = f32[32,128,128]{2,1,0:T(8,128)S(1)} fusion(f32[32,128,128]{2,1,0:T(8,128)S(1)} %broadcast_in_dim.2, s32[320]{0:T(512)S(1)} %get-tuple-element.7, f32[320,128,128]{2,1,0:T(8,128)} %copy.12), kind=kCustom, calls=%fused_computation.1 | custom fusion | flops 5242880 | bytes 62915840 | tf_op jit(solution)/shard_map/scatter-add | solution.py:28
  151.4 0.0 copy-start.2
  151.4 1.3 copy-done.2
  152.8 0.0 reduce-scatter.2.cloned.1.call-update
  152.8 107.0 %all-reduce.2.cloned.1.call-done = f32[128,128]{0,1:T(8,128)} async-done(((f32[128,128]{0,1:T(8,128)}), f32[128,128]{0,1:T(8,128)}) %all-reduce.2.cloned.1.call-update) | async-done | bytes 65552 | tf_op jit(solution)/shard_map/psum | solution.py:15
  259.8 1.6 copy.13
  261.3 0.0 reduce-scatter.2.cloned.1.call-done
  261.3 1.5 convert_element_type.27
  262.9 0.0 copy-done.1
  (2 shorter events, 0.0 us)
Async XLA Ops:
  8.0 1.7 copy-start
  8.0 54.0 %all-gather.2.cloned.1.call-start = ((), (), s32[]{:S(2)}) async-start(), calls=%async_computation.1 | async-start | bytes 1114112 | tf_op jit(solution)/shard_map/all_gather | solution.py:16
  9.6 250.2 %all-reduce.2.cloned.1.call-start = ((), (), s32[]{:S(2)}) async-start(), calls=%async_computation.3 | async-start | bytes 131072 | tf_op jit(solution)/shard_map/psum | solution.py:15
  11.4 250.0 %reduce-scatter.2.cloned.1.call-start = ((), (), s32[]{:S(2)}) async-start(), calls=%async_computation.2 | async-start | bytes 2228224 | tf_op jit(solution)/shard_map/reduce_scatter | solution.py:30
  109.4 153.4 %copy-start.1 = (bf16[256,128]{1,0:T(8,128)(2,1)S(1)}, bf16[256,128]{1,0:T(8,128)(2,1)}, u32[]{:S(2)}) copy-start(bf16[256,128]{1,0:T(8,128)(2,1)} %param.9) | copy-start | bytes 196612
  151.4 1.4 copy-start.2
Sparse Core Ops, SparseCore 0:
  11.9 50.1 all-gather.1
  152.9 57.1 reduce-scatter.1
Sparse Core Ops, SparseCore 1:
  16.2 243.5 all-reduce.1
where the time goes:
time: 272 us; the launch traced here: 270 us
  waiting for transfers between devices  156 us (57%)
  other arithmetic  45.8 us (17%)
  local copies, waits for them, and re-layouts  35 us (13%)
  matrix products  16.9 us (6%)
  between operations  16.2 us (6%)
    psum x1, waiting for transfers between devices, local(): weight_grad = lax.psum(term, ('row', 'col'))  107 us
    all_gather x1, waiting for transfers between devices, local(): grad_rows = lax.all_gather(pre_grad, 'col', axis=0, tiled=True)  49.2 us
    scatter-add x1, other arithmetic, local(): jax.ops.segment_sum(live_products, column_ids, num_segments=column_tiles)  42 us
    mul x1, local copies, waits for them, and re-layouts, local(): live_products = products * alive[:, None, None]  21.1 us
    dot_general x1, matrix products, local(): jnp.einsum('kab,kaf->kbf', values, gathered, preferred_element_type=jnp.f...  13.6 us
    gather x1, local copies, waits for them, and re-layouts, local(): gathered = panel_tiles[coords[:, 0]]  10.7 us
  transfers between devices with their start and end apart: 3, of which 2 were waited for; matrix products, arithmetic and copies ran while one was open for 35% of the time, Pallas kernels for 0%

commit v1 on v0

v1 whole, which is shorter than its diff:
```python
import functools

import jax
import jax.numpy as jnp
from jax import lax
from jax.experimental import pallas as pl
from jax.experimental.pallas import tpu as pltpu
from jax.sharding import PartitionSpec as P

MESH = pl.DeviceIdType.MESH
F32 = jnp.float32
BF16 = jnp.bfloat16

TILE = 128
SLOTS = 320
COLS = 32
HALF = 64
PAIRS = SLOTS // 2 + COLS // 2
LANES = 384
UNROLL = 8
CHUNKS = 4


def order_slots(coords, count):
    def total(condition, value, axis):
        return jnp.sum(jnp.where(condition, value, 0), axis=axis, keepdims=True)

    def iota(shape, axis):
        return lax.broadcasted_iota(jnp.int32, shape, axis)

    square = (SLOTS, SLOTS)
    down, across = iota(square, 0), iota(square, 1)
    live = iota((1, SLOTS), 1) < jnp.broadcast_to(count, (1, SLOTS))
    row = coords[0:1, :]
    key = jnp.where(live, coords[1:2, :], COLS)
    key_all = jnp.broadcast_to(key, square)
    key_down = total(down == across, key_all, 1)
    row_down = total(down == across, jnp.broadcast_to(row, square), 1)
    rank = total((key_down == key_all) & (across < down), 1, 1)

    member = key_down == iota((SLOTS, 128), 1)
    count_lane = total(member, 1, 0)
    count_down = total(jnp.broadcast_to(key, (COLS, SLOTS)) == iota((COLS, SLOTS), 0), 1, 1)
    padded_lane = (count_lane + 1) // 2 * 2
    padded_down = (count_down + 1) // 2 * 2
    low, high = iota((COLS, 128), 0), iota((COLS, 128), 1)
    start_lane = total(low < high, padded_down, 0)
    start_down = total(high < low, padded_lane, 1)

    place = jnp.where(key_down < COLS, total(member, start_lane, 1) + rank, -1)
    payload = iota((SLOTS, 1), 0) * 64 + row_down - COLS
    packed = COLS + total(place == iota((SLOTS, LANES), 1), payload, 0)

    pair = 2 * iota((COLS, LANES), 1)
    keep = 1 - total((start_down == pair) & (count_down > 0), 1, 0)
    last = jnp.where(count_lane > 0, (start_lane + padded_lane) // 2 - 1, PAIRS)
    return packed, keep, last


def kernel(
    out_grad, relu_mask, saved_agg, weight, tile_values, coords, count, input_grad, weight_grad,
    og, rm, sa, wt, tiles, xy, ct, meta_v, meta,
    agg0, agg1, run0, run1, xsend, xrecv, zsend, zrecv, own, term, areceived, breceived, creceived,
    load_sem, tile_sem, first_recv, second_recv, gather_send,
    xs_sem, xr_sem, zs_sem, zr_sem, w_send, w_recv,
):
    row, col = lax.axis_index("row"), lax.axis_index("col")
    z, core, x, y = row // 2, row % 2, col // 4, col % 4

    def at(xx, yy):
        return (row, xx % 4 * 4 + yy % 4)

    def up(d):
        return ((z + d) % 8 * 2 + core, col)

    partner = (z * 2 + 1 - core, col)
    plane = [(a, b) for a in range(4) for b in range(4) if a or b]

    barrier = pltpu.get_barrier_semaphore()
    for a, b in plane:
        pl.semaphore_signal(barrier, inc=1, device_id=at(x + a, y + b), device_id_type=MESH)
    for d in range(1, 8):
        pl.semaphore_signal(barrier, inc=1, device_id=up(d), device_id_type=MESH)
    pl.semaphore_signal(barrier, inc=1, device_id=partner, device_id_type=MESH)

    loads = [
        pltpu.make_async_copy(src, dst, load_sem.at[i])
        for i, (src, dst) in enumerate(
            ((out_grad, og), (relu_mask, rm), (weight, wt), (saved_agg, sa), (coords, xy), (count, ct))
        )
    ]
    for load in loads:
        load.start()
    step = SLOTS // CHUNKS
    tile_loads = [
        pltpu.make_async_copy(
            tile_values.at[0, 0, pl.ds(i * step, step)], tiles.at[pl.ds(i * step, step)], tile_sem.at[i]
        )
        for i in range(CHUNKS)
    ]
    for load in tile_loads:
        load.start()

    aggs, runs = (agg0, agg1), (run0, run1)
    for agg in aggs:
        agg[COLS] = jnp.zeros((HALF, TILE), BF16)
    for run in runs:
        run[PAIRS] = jnp.zeros((HALF, TILE), F32)

    for load in loads[:3]:
        load.wait()
    pre = (og[...].astype(F32) * rm[...].astype(F32)).astype(BF16)
    mine = lax.dot_general(wt[...], pre, (((1,), (1,)), ((), ())), preferred_element_type=F32).astype(BF16)
    for h in range(2):
        for e in range(2):
            aggs[h][2 * col + e] = mine[h * HALF : (h + 1) * HALF, e * TILE : (e + 1) * TILE]

    pl.semaphore_wait(barrier, len(plane) + 8)

    def toward(e, phase, d):
        return at(x + d, y) if (e + phase) % 2 == 0 else at(x, y + d)

    def piece(e, d):
        a, b = ((x - d) % 4, y) if e == 0 else (x, (y - d) % 4)
        return 2 * (a * 4 + b) + e

    def gather_copy(h, r, recv, target):
        block = aggs[h].at[r]
        return pltpu.make_async_remote_copy(
            src_ref=block, dst_ref=block, send_sem=gather_send.at[h], recv_sem=recv, device_id=target, device_id_type=MESH
        )

    def second(h, e, r):
        for d in (2, 1, 3):
            gather_copy(h, r, second_recv.at[h], toward(e, 1, d)).start()

    for h in range(2):
        for e in range(2):
            for d in (2, 1, 3):
                gather_copy(h, 2 * col + e, first_recv.at[h * 6 + e * 3 + d - 1], toward(e, 0, d)).start()
        for e in range(2):
            second(h, e, 2 * col + e)

    loads[3].wait()
    term[...] = lax.dot_general(sa[...], pre, (((0,), (0,)), ((), ())), preferred_element_type=F32)
    areceived[col] = term[pl.ds(pl.multiple_of(col * 8, 8), 8), :]
    for a, b in plane:
        target = (x + a) % 4 * 4 + (y + b) % 4
        pltpu.make_async_remote_copy(
            src_ref=term.at[pl.ds(pl.multiple_of(target * 8, 8), 8)], dst_ref=areceived.at[col],
            send_sem=w_send.at[0], recv_sem=w_recv.at[0], device_id=(row, target), device_id_type=MESH,
        ).start()

    loads[4].wait()
    loads[5].wait()
    packed, keep, last = order_slots(xy[...], ct[...])
    meta_v[...] = jnp.full((8, LANES), PAIRS, jnp.int32)
    meta_v[0:1, :] = packed
    meta_v[1:2, :] = keep
    meta_v[2:3, 0:128] = last
    to_scalar = pltpu.make_async_copy(meta_v, meta, load_sem.at[6])
    to_scalar.start()

    for h in range(2):
        for e in range(2):
            for d in range(1, 4):
                r = piece(e, d)
                gather_copy(h, r, first_recv.at[h * 6 + e * 3 + d - 1], toward(e, 0, d)).wait_recv()
                second(h, e, r)
    to_scalar.wait()
    for load in tile_loads:
        load.wait()

    def gathered(h):
        part = aggs[h].at[pl.ds(0, 24)]
        pltpu.make_async_copy(part, part, second_recv.at[h]).wait()

    def products(h):
        agg, run = aggs[h], runs[h]

        def body(t, total):
            for u in range(UNROLL):
                q = t * UNROLL + u
                a, b = meta[0, 2 * q], meta[0, 2 * q + 1]
                left = jnp.concatenate([agg[a & 63], agg[b & 63]], axis=1)
                right = jnp.concatenate([tiles[a >> 6], tiles[b >> 6]], axis=0)
                total = total * meta[1, q].astype(F32) + jnp.dot(left, right, preferred_element_type=F32)
                run[q] = total
            return total

        lax.fori_loop(0, PAIRS // UNROLL, body, jnp.zeros((HALF, TILE), F32))

    def swap(h):
        return pltpu.make_async_remote_copy(
            src_ref=xsend.at[h], dst_ref=xrecv.at[h], send_sem=xs_sem.at[h], recv_sem=xr_sem.at[h],
            device_id=partner, device_id_type=MESH,
        )

    def scatter_first(h):
        for d in range(8):
            for e in range(2):
                xsend[h, d, e] = runs[h][meta[2, d * 4 + (1 - core) * 2 + e]].astype(BF16)
        swap(h).start()

    def scatter_copy(h, d):
        return pltpu.make_async_remote_copy(
            src_ref=zsend.at[h, d - 1], dst_ref=zrecv.at[h, d - 1], send_sem=zs_sem.at[h], recv_sem=zr_sem.at[h],
            device_id=up(d), device_id_type=MESH,
        )

    def scatter_second(h):
        swap(h).wait_recv()
        for d in (4, 3, 5, 2, 6, 1, 7, 0):
            goal = (z + d) % 8
            for e in range(2):
                value = runs[h][meta[2, goal * 4 + core * 2 + e]] + xrecv[h, goal, e].astype(F32)
                if d:
                    zsend[h, d - 1, e] = value.astype(BF16)
                else:
                    own[h, e] = value
            if d:
                scatter_copy(h, d).start()

    def plain(ref, sem):
        return pltpu.make_async_copy(ref, ref, sem)

    gathered(0)
    plain(areceived.at[pl.ds(0, 15)], w_recv.at[0]).wait()
    mysum = areceived[0]
    for i in range(1, 16):
        mysum = mysum + areceived[i]
    breceived[z] = mysum
    for d in range(1, 8):
        pltpu.make_async_remote_copy(
            src_ref=breceived.at[z], dst_ref=breceived.at[z], send_sem=w_send.at[1], recv_sem=w_recv.at[1],
            device_id=up(d), device_id_type=MESH,
        ).start()

    products(0)
    scatter_first(0)

    plain(breceived.at[pl.ds(0, 7)], w_recv.at[1]).wait()
    mysum = breceived[0]
    for i in range(1, 8):
        mysum = mysum + breceived[i]
    creceived[0] = mysum
    half_sum = pltpu.make_async_remote_copy(
        src_ref=creceived.at[0], dst_ref=creceived.at[1], send_sem=w_send.at[2], recv_sem=w_recv.at[2],
        device_id=partner, device_id_type=MESH,
    )
    half_sum.start()
    scatter_second(0)

    gathered(1)
    products(1)
    scatter_first(1)

    half_sum.wait_recv()
    mine_rows = pl.ds(pl.multiple_of(col * 8, 8), 8)
    weight_grad[mine_rows, :] = creceived[0] + creceived[1]
    for a, b in plane:
        pltpu.make_async_remote_copy(
            src_ref=weight_grad.at[mine_rows], dst_ref=weight_grad.at[mine_rows],
            send_sem=w_send.at[3], recv_sem=w_recv.at[3], device_id=at(x + a, y + b), device_id_type=MESH,
        ).start()
    scatter_second(1)

    halves = []
    for h in range(2):
        plain(zrecv.at[h], zr_sem.at[h]).wait()
        pair = []
        for e in range(2):
            value = own[h, e]
            for d in range(7):
                value = value + zrecv[h, d, e].astype(F32)
            pair.append(value)
        halves.append(pair)
    for e in range(2):
        whole = jnp.concatenate([halves[0][e], halves[1][e]], axis=0)
        input_grad[e * TILE : (e + 1) * TILE, :] = whole.T.astype(BF16)

    plain(weight_grad.at[pl.ds(0, 120)], w_recv.at[3]).wait()
    plain(term.at[pl.ds(0, 120)], w_send.at[0]).wait()
    plain(breceived.at[pl.ds(0, 7)], w_send.at[1]).wait()
    half_sum.wait_send()
    plain(term.at[pl.ds(0, 120)], w_send.at[3]).wait()
    for h in range(2):
        part = aggs[h].at[pl.ds(0, 30)]
        plain(part, gather_send.at[h]).wait()
        swap(h).wait_send()
        plain(zsend.at[h], zs_sem.at[h]).wait()


def local(out_grad, relu_mask, saved_agg, weight, tile_values, tile_coords, tile_count):
    nodes = out_grad.shape[0]
    vmem, dma = pltpu.VMEM, pltpu.SemaphoreType.DMA
    return pl.pallas_call(
        kernel,
        out_shape=(
            jax.ShapeDtypeStruct((nodes, TILE), BF16),
            jax.ShapeDtypeStruct((TILE, TILE), F32),
        ),
        in_specs=[pl.BlockSpec(memory_space=pl.ANY)] * 7,
        out_specs=(pl.BlockSpec(memory_space=pltpu.VMEM), pl.BlockSpec(memory_space=pltpu.VMEM)),
        scratch_shapes=[
            vmem((nodes, TILE), BF16),
            vmem((nodes, TILE), BF16),
            vmem((nodes, TILE), BF16),
            vmem((TILE, TILE), BF16),
            vmem((SLOTS, TILE, TILE), BF16),
            vmem((2, SLOTS), jnp.int32),
            vmem((1, 1), jnp.int32),
            vmem((8, LANES), jnp.int32),
            pltpu.SMEM((8, LANES), jnp.int32),
            vmem((COLS + 1, HALF, TILE), BF16),
            vmem((COLS + 1, HALF, TILE), BF16),
            vmem((PAIRS + 1, HALF, TILE), F32),
            vmem((PAIRS + 1, HALF, TILE), F32),
            vmem((2, 8, 2, HALF, TILE), BF16),
            vmem((2, 8, 2, HALF, TILE), BF16),
            vmem((2, 7, 2, HALF, TILE), BF16),
            vmem((2, 7, 2, HALF, TILE), BF16),
            vmem((2, 2, HALF, TILE), F32),
            vmem((TILE, TILE), F32),
            vmem((16, 8, TILE), F32),
            vmem((8, 8, TILE), F32),
            vmem((2, 8, TILE), F32),
            dma((7,)),
            dma((CHUNKS,)),
            dma((12,)),
            dma((2,)),
            dma((2,)),
            dma((2,)),
            dma((2,)),
            dma((2,)),
            dma((2,)),
            dma((4,)),
            dma((4,)),
        ],
        compiler_params=pltpu.CompilerParams(
            collective_id=0, has_side_effects=True, vmem_limit_bytes=48 * 1024 * 1024
        ),
    )(out_grad, relu_mask, saved_agg, weight, tile_values, tile_coords[0, 0].T, tile_count)


def solution(mesh):
    in_specs = (
        P(("row", "col"), None),
        P(("row", "col"), None),
        P(("row", "col"), None),
        P(),
        P("row", "col", None, None, None),
        P("row", "col", None, None),
        P("row", "col"),
    )
    out_specs = (P(("col", "row"), None), P())
    return jax.shard_map(local, mesh=mesh, in_specs=in_specs, out_specs=out_specs, check_vma=False)
```

time: 272 us -> 45.6 us (0.17)
  waiting for transfers between devices: 156 us -> 0 us
  other arithmetic: 45.8 us -> 0 us
  Pallas kernels: 0 us -> 38.8 us
  local copies, waits for them, and re-layouts: 35 us -> 5.21 us
  matrix products: 16.9 us -> 0 us
  between operations: 16.2 us -> 1.3 us
    psum x1 -> x0, waiting for transfers between devices: 107 us -> none  [local(): weight_grad = lax.psum(term, ('row', 'col'))]
    all_gather x1 -> x0, waiting for transfers between devices: 49.2 us -> none  [local(): grad_rows = lax.all_gather(pre_grad, 'col', axis=0, tiled=True)]
    scatter-add x1 -> x0, other arithmetic: 42 us -> none  [local(): jax.ops.segment_sum(live_products, column_ids, num_segments=column_tiles)]
    pallas_call x0 -> x1, Pallas kernels: none -> 38.8 us  [local(): pl.pallas_call(kernel, out_shape=(jax.ShapeDtypeStruct((nodes, TILE), BF1...]
    mul x1 -> x0, local copies, waits for them, and re-layouts: 21.1 us -> none  [local(): live_products = products * alive[:, None, None]]
    dot_general x3 -> x0, matrix products: 16.9 us -> none  [the longest x1 13.6 us: local(): jnp.einsum('kab,kaf->kbf', values, gathered, preferred_element_type=jnp.f...]
    gather x1 -> x0, local copies, waits for them, and re-layouts: 10.7 us -> none  [local(): gathered = panel_tiles[coords[:, 0]]]
    convert_element_type x3 -> x0, other arithmetic: 3.07 us -> none  [the longest x1 1.54 us: local(): input_grad = summed.astype(jnp.bfloat16)]
  transfers between devices with their start and end apart: 3 -> 0, of which waited for: 2 -> 0; matrix products, arithmetic and copies ran while one was open for 35% -> 0% of each run, Pallas kernels for 0% -> 0%
where the time goes in v1:
time: 45.6 us; the launch traced here: 45.3 us
  Pallas kernels  38.8 us (85%)
  local copies, waits for them, and re-layouts  5.21 us (11%)
  between operations  1.3 us (3%)
    pallas_call x1, Pallas kernels, local(): pl.pallas_call(kernel, out_shape=(jax.ShapeDtypeStruct((nodes, TILE), BF1...  38.8 us
    unnamed x12, local copies, waits for them, and re-layouts  5.21 us

profile of v1, /device:TPU:1, one launch (start us, length us, event | category | flops | bytes accessed | tf_op | source)
XLA Modules:
  0.0 45.3 jit_solution(12388498923737660551)
XLA Ops:
  1.3 0.0 copy-start
  1.3 0.8 %copy-done = bf16[256,128]{1,0:T(8,128)(2,1)S(1)} copy-done((bf16[256,128]{1,0:T(8,128)(2,1)S(1)}, bf16[256,128]{1,0:T(8,128)(2,1)}, u32[]{:S(2)}) %copy-start) | copy-done | bytes 65560
  2.1 0.0 copy-start.1
  2.1 0.8 %copy-done.1 = bf16[256,128]{1,0:T(8,128)(2,1)S(1)} copy-done((bf16[256,128]{1,0:T(8,128)(2,1)S(1)}, bf16[256,128]{1,0:T(8,128)(2,1)}, u32[]{:S(2)}) %copy-start.1) | copy-done | bytes 65560
  3.0 0.0 copy-start.2
  3.0 0.8 %copy-done.2 = bf16[256,128]{1,0:T(8,128)(2,1)S(1)} copy-done((bf16[256,128]{1,0:T(8,128)(2,1)S(1)}, bf16[256,128]{1,0:T(8,128)(2,1)}, u32[]{:S(2)}) %copy-start.2) | copy-done | bytes 65560
  3.8 0.0 copy-start.3
  3.8 0.8 %copy-done.3 = bf16[128,128]{1,0:T(8,128)(2,1)S(1)} copy-done((bf16[128,128]{1,0:T(8,128)(2,1)S(1)}, bf16[128,128]{1,0:T(8,128)(2,1)}, u32[]{:S(2)}) %copy-start.3) | copy-done | bytes 32792
  4.6 0.0 copy-start.4
  4.6 0.7 %copy-done.4 = s32[1,1,320,2]{2,3,1,0:T(2,128)S(1)} copy-done((s32[1,1,320,2]{2,3,1,0:T(2,128)S(1)}, s32[1,1,320,2]{2,3,1,0:T(2,128)}, u32[]{:S(2)}) %copy-start.4) | copy-done | bytes 2584
  5.2 38.8 %shard_map.86 = (bf16[256,128]{1,0:T(8,128)(2,1)S(1)}, f32[128,128]{1,0:T(8,128)S(1)}) custom-call(bf16[256,128]{1,0:T(8,128)(2,1)S(1)} %copy-done, bf16[256,128]{1,0:T(8,128)(2,1)S(1)} %copy-done.1, bf16[256,128]{1,0:T(8,128)(2,1)S(1)} %copy-done.2, bf16[128,128]{1,0:T(8,128)(2,1)S(1)} %copy-done.3, bf16[1,1,320,128,128]{4,3,2,1,0:T(8,128)(2,1)} %tile_values.1, ...), custom_call_target="tpu_custom_call" | custom-call | tf_op jit(solution)/shard_map/pallas_call | solution.py:297
  44.0 0.6 %copy.12 = bf16[256,128]{1,0:T(8,128)(2,1)} copy(bf16[256,128]{1,0:T(8,128)(2,1)S(1)} %get-tuple-element.4) | data formatting | bytes 131072
  44.7 0.6 %copy.13 = f32[128,128]{1,0:T(8,128)} copy(f32[128,128]{1,0:T(8,128)S(1)} %get-tuple-element.5) | data formatting | bytes 131072
Async XLA Ops:
  1.3 0.8 %copy-start = (bf16[256,128]{1,0:T(8,128)(2,1)S(1)}, bf16[256,128]{1,0:T(8,128)(2,1)}, u32[]{:S(2)}) copy-start(bf16[256,128]{1,0:T(8,128)(2,1)} %out_grad.1) | copy-start | bytes 196612
  2.1 0.8 %copy-start.1 = (bf16[256,128]{1,0:T(8,128)(2,1)S(1)}, bf16[256,128]{1,0:T(8,128)(2,1)}, u32[]{:S(2)}) copy-start(bf16[256,128]{1,0:T(8,128)(2,1)} %relu_mask.1) | copy-start | bytes 196612
  3.0 0.8 %copy-start.2 = (bf16[256,128]{1,0:T(8,128)(2,1)S(1)}, bf16[256,128]{1,0:T(8,128)(2,1)}, u32[]{:S(2)}) copy-start(bf16[256,128]{1,0:T(8,128)(2,1)} %saved_agg.1) | copy-start | bytes 196612
  3.8 0.8 %copy-start.3 = (bf16[128,128]{1,0:T(8,128)(2,1)S(1)}, bf16[128,128]{1,0:T(8,128)(2,1)}, u32[]{:S(2)}) copy-start(bf16[128,128]{1,0:T(8,128)(2,1)} %weight.1) | copy-start | bytes 98308
  4.6 0.7 %copy-start.4 = (s32[1,1,320,2]{2,3,1,0:T(2,128)S(1)}, s32[1,1,320,2]{2,3,1,0:T(2,128)}, u32[]{:S(2)}) copy-start(s32[1,1,320,2]{2,3,1,0:T(2,128)} %param.12) | copy-start | bytes 7684

commit v2 on v1

v2 whole, which is shorter than its diff:
```python
import functools

import jax
import jax.numpy as jnp
from jax import lax
from jax.experimental import pallas as pl
from jax.experimental.pallas import tpu as pltpu
from jax.sharding import PartitionSpec as P

MESH = pl.DeviceIdType.MESH
F32 = jnp.float32
BF16 = jnp.bfloat16

TILE = 128
SLOTS = 320
COLS = 32
HALF = 64
PAIRS = SLOTS // 2 + COLS // 2
LANES = 384
UNROLL = 44
CHUNKS = 4


def order_slots(coords, count):
    def total(condition, value, axis):
        return jnp.sum(jnp.where(condition, value, 0), axis=axis, keepdims=True)

    def iota(shape, axis):
        return lax.broadcasted_iota(jnp.int32, shape, axis)

    square = (SLOTS, SLOTS)
    down, across = iota(square, 0), iota(square, 1)
    live = iota((1, SLOTS), 1) < jnp.broadcast_to(count, (1, SLOTS))
    row = coords[0:1, :]
    key = jnp.where(live, coords[1:2, :], COLS)
    key_all = jnp.broadcast_to(key, square)
    key_down = total(down == across, key_all, 1)
    row_down = total(down == across, jnp.broadcast_to(row, square), 1)
    rank = total((key_down == key_all) & (across < down), 1, 1)

    member = key_down == iota((SLOTS, 128), 1)
    count_lane = total(member, 1, 0)
    count_down = total(jnp.broadcast_to(key, (COLS, SLOTS)) == iota((COLS, SLOTS), 0), 1, 1)
    padded_lane = (count_lane + 1) // 2 * 2
    padded_down = (count_down + 1) // 2 * 2
    low, high = iota((COLS, 128), 0), iota((COLS, 128), 1)
    start_lane = total(low < high, padded_down, 0)
    start_down = total(high < low, padded_lane, 1)

    place = jnp.where(key_down < COLS, total(member, start_lane, 1) + rank, -1)
    payload = iota((SLOTS, 1), 0) * 64 + row_down - COLS
    packed = COLS + total(place == iota((SLOTS, LANES), 1), payload, 0)

    pair = 2 * iota((COLS, LANES), 1)
    keep = 1 - total((start_down == pair) & (count_down > 0), 1, 0)
    last = jnp.where(count_lane > 0, (start_lane + padded_lane) // 2 - 1, PAIRS)
    return packed, keep, last


def kernel(
    out_grad, relu_mask, saved_agg, weight, tile_values, coords, count, input_grad, weight_grad,
    og, rm, sa, wt, tiles, xy, ct, meta_v, meta,
    agg0, agg1, run0, run1, xsend, xrecv, zsend, zrecv, own, term, w1, w1s, w2, w3, w4,
    load_sem, tile_sem, first_recv, second_recv, gather_send,
    xs_sem, xr_sem, zs_sem, zr_sem, w_send, w_recv, near_sem,
):
    row, col = lax.axis_index("row"), lax.axis_index("col")
    z, core, x, y = row // 2, row % 2, col // 4, col % 4

    def at(xx, yy):
        return (row, xx % 4 * 4 + yy % 4)

    turn = 1 - 2 * core

    def up(d):
        return ((z + d + 8) % 8 * 2 + core, col)

    partner = (z * 2 + 1 - core, col)

    barrier = pltpu.get_barrier_semaphore()
    peers = [at(x + d, y) for d in (1, 2, 3)] + [at(x, y + d) for d in (1, 2, 3)] + [up(d) for d in (1, 2, 6, 7)] + [partner]
    for peer in peers:
        pl.semaphore_signal(barrier, inc=1, device_id=peer, device_id_type=MESH)

    loads = [
        pltpu.make_async_copy(src, dst, load_sem.at[i])
        for i, (src, dst) in enumerate(
            ((out_grad, og), (relu_mask, rm), (weight, wt), (saved_agg, sa), (coords, xy), (count, ct))
        )
    ]
    for load in loads:
        load.start()
    step = SLOTS // CHUNKS
    tile_loads = [
        pltpu.make_async_copy(
            tile_values.at[0, 0, pl.ds(i * step, step)], tiles.at[pl.ds(i * step, step)], tile_sem.at[i]
        )
        for i in range(CHUNKS)
    ]
    for load in tile_loads:
        load.start()

    aggs, runs = (agg0, agg1), (run0, run1)
    for agg in aggs:
        agg[COLS] = jnp.zeros((HALF, TILE), BF16)
    for run in runs:
        run[PAIRS] = jnp.zeros((HALF, TILE), F32)

    for load in loads[:3]:
        load.wait()
    pre = (og[...].astype(F32) * rm[...].astype(F32)).astype(BF16)
    mine = lax.dot_general(wt[...], pre, (((1,), (1,)), ((), ())), preferred_element_type=F32).astype(BF16)
    for h in range(2):
        for e in range(2):
            aggs[h][2 * col + e] = mine[h * HALF : (h + 1) * HALF, e * TILE : (e + 1) * TILE]

    pl.semaphore_wait(barrier, len(peers))
    for d in (2, 6):
        pl.semaphore_signal(near_sem, inc=1, device_id=up(d), device_id_type=MESH)

    def toward(e, phase, d):
        return at(x + d, y) if (e + phase) % 2 == 0 else at(x, y + d)

    def piece(e, d):
        a, b = ((x - d) % 4, y) if e == 0 else (x, (y - d) % 4)
        return 2 * (a * 4 + b) + e

    def gather_copy(h, r, recv, target):
        block = aggs[h].at[r]
        return pltpu.make_async_remote_copy(
            src_ref=block, dst_ref=block, send_sem=gather_send.at[h], recv_sem=recv, device_id=target, device_id_type=MESH
        )

    def second(h, e, r):
        for d in (2, 1, 3):
            gather_copy(h, r, second_recv.at[h], toward(e, 1, d)).start()

    for h in range(2):
        for e in range(2):
            for d in (2, 1, 3):
                gather_copy(h, 2 * col + e, first_recv.at[h * 6 + e * 3 + d - 1], toward(e, 0, d)).start()
        for e in range(2):
            second(h, e, 2 * col + e)

    loads[3].wait()
    term[...] = lax.dot_general(sa[...], pre, (((0,), (0,)), ((), ())), preferred_element_type=F32)

    def rows(start, size):
        return pl.ds(pl.multiple_of(start, 8), size)

    def share(i, src, dst, target):
        return pltpu.make_async_remote_copy(
            src_ref=src, dst_ref=dst, send_sem=w_send.at[i], recv_sem=w_recv.at[i], device_id=target, device_id_type=MESH
        )

    def plain(ref, sem):
        return pltpu.make_async_copy(ref, ref, sem)

    def added(ref, n):
        value = ref[0]
        for i in range(1, n):
            value = value + ref[i]
        return value

    w1[x] = term[rows(x * 32, 32), :]
    for d in (2, 1, 3):
        share(0, term.at[rows((x + d) % 4 * 32, 32)], w1.at[x], at(x + d, y)).start()

    loads[4].wait()
    loads[5].wait()
    packed, keep, last = order_slots(xy[...], ct[...])
    meta_v[...] = jnp.full((8, LANES), PAIRS, jnp.int32)
    meta_v[0:1, :] = packed
    meta_v[1:2, :] = keep
    meta_v[2:3, 0:128] = last
    to_scalar = pltpu.make_async_copy(meta_v, meta, load_sem.at[6])
    to_scalar.start()

    for h in range(2):
        for d in (1, 3, 2):
            for e in range(2):
                r = piece(e, d)
                gather_copy(h, r, first_recv.at[h * 6 + e * 3 + d - 1], toward(e, 0, d)).wait_recv()
                second(h, e, r)

    plain(w1.at[pl.ds(0, 3)], w_recv.at[0]).wait()
    w1s[...] = added(w1, 4)
    w2[y] = w1s[rows(y * 8, 8), :]
    for d in (2, 1, 3):
        share(1, w1s.at[rows((y + d) % 4 * 8, 8)], w2.at[y], at(x, y + d)).start()

    to_scalar.wait()
    for load in tile_loads:
        load.wait()

    def gathered(h):
        plain(aggs[h].at[pl.ds(0, 24)], second_recv.at[h]).wait()

    def products(h):
        agg, run = aggs[h], runs[h]

        def body(t, total):
            for u in range(UNROLL):
                q = t * UNROLL + u
                a, b = meta[0, 2 * q], meta[0, 2 * q + 1]
                left = jnp.concatenate([agg[a & 63], agg[b & 63]], axis=1)
                right = jnp.concatenate([tiles[a >> 6], tiles[b >> 6]], axis=0)
                total = total * meta[1, q].astype(F32) + jnp.dot(left, right, preferred_element_type=F32)
                run[q] = total
            return total

        lax.fori_loop(0, PAIRS // UNROLL, body, jnp.zeros((HALF, TILE), F32))

    def swap(h, far):
        part = pl.ds(5, 3) if far else pl.ds(0, 5)
        return pltpu.make_async_remote_copy(
            src_ref=xsend.at[h, part], dst_ref=xrecv.at[h, part], send_sem=xs_sem.at[h, int(far)],
            recv_sem=xr_sem.at[h, int(far)], device_id=partner, device_id_type=MESH,
        )

    def column(h, owner, k, e):
        return runs[h][meta[2, owner * 4 + k * 2 + e]]

    def scatter_swap(h):
        for far in (True, False):
            for slot in (6, 5, 7) if far else (0, 1, 3, 4, 2):
                for e in range(2):
                    xsend[h, slot, e] = column(h, (z + slot + 6) % 8, 1 - core, e).astype(BF16)
            swap(h, far).start()

    roles = (4, 3, -3, 1, -1, 2, -2)

    def scatter_copy(h, r):
        i, step = roles.index(r), {4: -2, 3: -1, -3: 1, 1: -1, -1: 1, 2: -2, -2: 2}[r]
        return pltpu.make_async_remote_copy(
            src_ref=zsend.at[h, i], dst_ref=zrecv.at[h, i], send_sem=zs_sem.at[h, i], recv_sem=zr_sem.at[h, i],
            device_id=up(turn * step), device_id_type=MESH,
        )

    def pair_sum(h, r, e):
        slot = (2 - turn * r + 8) % 8
        return column(h, (z - turn * r + 8) % 8, core, e) + xrecv[h, slot, e].astype(F32)

    def scatter_near(h):
        swap(h, True).wait_recv()
        for r in roles[:5]:
            if r == 1:
                swap(h, False).wait_recv()
            for e in range(2):
                zsend[h, roles.index(r), e] = pair_sum(h, r, e).astype(BF16)
            scatter_copy(h, r).start()
        for i, r in enumerate((2, -2, 0)):
            for e in range(2):
                own[h, i, e] = pair_sum(h, r, e)

    def scatter_far(h):
        for r, sources in ((2, (4, 3)), (-2, (-3,))):
            for q in sources:
                scatter_copy(h, q).wait_recv()
            for e in range(2):
                value = own[h, 0 if r == 2 else 1, e]
                for q in sources:
                    value = value + zrecv[h, roles.index(q), e].astype(F32)
                zsend[h, roles.index(r), e] = value.astype(BF16)
            scatter_copy(h, r).start()

    def scattered(h):
        result = []
        for r in roles[3:]:
            scatter_copy(h, r).wait_recv()
        for e in range(2):
            value = own[h, 2, e]
            for i in range(3, 7):
                value = value + zrecv[h, i, e].astype(F32)
            result.append(value)
        return result

    gathered(0)
    plain(w2.at[pl.ds(0, 3)], w_recv.at[1]).wait()
    w3[core] = added(w2, 4)
    share(2, w3.at[core], w3.at[core], partner).start()

    products(0)
    scatter_swap(0)

    share(2, w3.at[core], w3.at[1 - core], partner).wait_recv()
    w4[z] = w3[0] + w3[1]
    pl.semaphore_wait(near_sem, 2)
    for d in (4, 3, 5, 2, 6, 1, 7):
        share(3, w4.at[z], w4.at[z], up(d)).start()
    scatter_near(0)

    gathered(1)
    products(1)
    scatter_swap(1)
    scatter_far(0)
    scatter_near(1)

    plain(w4.at[pl.ds(0, 7)], w_recv.at[3]).wait()
    mine_rows = rows(x * 32 + y * 8, 8)
    weight_grad[mine_rows, :] = added(w4, 8)
    for d in (2, 1, 3):
        share(4, weight_grad.at[mine_rows], weight_grad.at[mine_rows], at(x, y + d)).start()
    first_half = scattered(0)
    scatter_far(1)
    plain(weight_grad.at[pl.ds(0, 24)], w_recv.at[4]).wait()
    line_rows = rows(x * 32, 32)
    for d in (2, 1, 3):
        share(5, weight_grad.at[line_rows], weight_grad.at[line_rows], at(x + d, y)).start()

    second_half = scattered(1)
    for e in range(2):
        whole = jnp.concatenate([first_half[e], second_half[e]], axis=0)
        input_grad[e * TILE : (e + 1) * TILE, :] = whole.T.astype(BF16)

    plain(weight_grad.at[pl.ds(0, 96)], w_recv.at[5]).wait()
    for i, size in enumerate((96, 24, 8, 56, 24, 96)):
        plain(term.at[pl.ds(0, size)], w_send.at[i]).wait()
    for h in range(2):
        plain(aggs[h].at[pl.ds(0, 30)], gather_send.at[h]).wait()
        for far in (True, False):
            swap(h, far).wait_send()
        for r in roles:
            scatter_copy(h, r).wait_send()


def local(out_grad, relu_mask, saved_agg, weight, tile_values, tile_coords, tile_count):
    nodes = out_grad.shape[0]
    vmem, dma = pltpu.VMEM, pltpu.SemaphoreType.DMA
    return pl.pallas_call(
        kernel,
        out_shape=(
            pltpu.VMEM((nodes, TILE), BF16),
            pltpu.VMEM((TILE, TILE), F32),
        ),
        in_specs=[pl.BlockSpec(memory_space=pltpu.HBM)] * 7,
        out_specs=(pl.BlockSpec(memory_space=pltpu.VMEM), pl.BlockSpec(memory_space=pltpu.VMEM)),
        scratch_shapes=[
            vmem((nodes, TILE), BF16),
            vmem((nodes, TILE), BF16),
            vmem((nodes, TILE), BF16),
            vmem((TILE, TILE), BF16),
            vmem((SLOTS, TILE, TILE), BF16),
            vmem((2, SLOTS), jnp.int32),
            vmem((1, 1), jnp.int32),
            vmem((8, LANES), jnp.int32),
            pltpu.SMEM((8, LANES), jnp.int32),
            vmem((COLS + 1, HALF, TILE), BF16),
            vmem((COLS + 1, HALF, TILE), BF16),
            vmem((PAIRS + 1, HALF, TILE), F32),
            vmem((PAIRS + 1, HALF, TILE), F32),
            vmem((2, 8, 2, HALF, TILE), BF16),
            vmem((2, 8, 2, HALF, TILE), BF16),
            vmem((2, 7, 2, HALF, TILE), BF16),
            vmem((2, 7, 2, HALF, TILE), BF16),
            vmem((2, 3, 2, HALF, TILE), F32),
            vmem((TILE, TILE), F32),
            vmem((4, 32, TILE), F32),
            vmem((32, TILE), F32),
            vmem((4, 8, TILE), F32),
            vmem((2, 8, TILE), F32),
            vmem((8, 8, TILE), F32),
            dma((7,)),
            dma((CHUNKS,)),
            dma((12,)),
            dma((2,)),
            dma((2,)),
            dma((2, 2)),
            dma((2, 2)),
            dma((2, 7)),
            dma((2, 7)),
            dma((6,)),
            dma((6,)),
            pltpu.SemaphoreType.REGULAR,
        ],
        compiler_params=pltpu.CompilerParams(
            collective_id=0, has_side_effects=True, vmem_limit_bytes=48 * 1024 * 1024
        ),
    )(*[
        pltpu.with_memory_space_constraint(array, pltpu.HBM)
        for array in (out_grad, relu_mask, saved_agg, weight, tile_values, tile_coords[0, 0].T)
    ], tile_count)


def solution(mesh):
    in_specs = (
        P(("row", "col"), None),
        P(("row", "col"), None),
        P(("row", "col"), None),
        P(),
        P("row", "col", None, None, None),
        P("row", "col", None, None),
        P("row", "col"),
    )
    out_specs = (P(("col", "row"), None), P())
    return jax.shard_map(local, mesh=mesh, in_specs=in_specs, out_specs=out_specs, check_vma=False)
```

time: 45.6 us -> 38.8 us (0.85)
  local copies, waits for them, and re-layouts: 5.21 us -> 1.26 us
  Pallas kernels: 38.8 us -> 36.2 us
    unnamed x12 -> x2, local copies, waits for them, and re-layouts: 5.21 us -> 1.26 us
    pallas_call x1, Pallas kernels: 38.8 us -> 36.2 us  [local(): pl.pallas_call(kernel, out_shape=(pltpu.VMEM((nodes, TILE), BF16), pltpu....]
where the time goes in v2:
time: 38.8 us; the launch traced here: 38.7 us
  Pallas kernels  36.2 us (93%)
  between operations  1.29 us (3%)
  local copies, waits for them, and re-layouts  1.26 us (3%)
    pallas_call x1, Pallas kernels, local(): pl.pallas_call(kernel, out_shape=(pltpu.VMEM((nodes, TILE), BF16), pltpu....  36.2 us
    unnamed x2, local copies, waits for them, and re-layouts  1.26 us

profile of v2, /device:TPU:1, one launch (start us, length us, event | category | flops | bytes accessed | tf_op | source)
XLA Modules:
  0.0 38.7 jit_solution(11390818829259487430)
XLA Ops:
  1.3 36.2 %shard_map.86 = (bf16[256,128]{1,0:T(8,128)(2,1)S(1)}, f32[128,128]{1,0:T(8,128)S(1)}) custom-call(bf16[256,128]{1,0:T(8,128)(2,1)} %out_grad.1, bf16[256,128]{1,0:T(8,128)(2,1)} %relu_mask.1, bf16[256,128]{1,0:T(8,128)(2,1)} %saved_agg.1, bf16[128,128]{1,0:T(8,128)(2,1)} %weight.1, bf16[1,1,320,128,128]{4,3,2,1,0:T(8,128)(2,1)} %tile_values.1, ...), custom_call_target="tpu_custom_call" | custom-call | tf_op jit(solution)/shard_map/pallas_call | solution.py:330
  37.4 0.6 %copy.11 = bf16[256,128]{1,0:T(8,128)(2,1)} copy(bf16[256,128]{1,0:T(8,128)(2,1)S(1)} %get-tuple-element.2) | data formatting | bytes 131072
  38.1 0.6 %copy.12 = f32[128,128]{1,0:T(8,128)} copy(f32[128,128]{1,0:T(8,128)S(1)} %get-tuple-element.3) | data formatting | bytes 131072

commit v3 on v2

--- a/solution.py
+++ b/solution.py
@@ -17,7 +17,7 @@
 HALF = 64
 PAIRS = SLOTS // 2 + COLS // 2
 LANES = 384
-UNROLL = 44
+UNROLL = 88
 CHUNKS = 4
 
 
@@ -162,9 +162,8 @@
             value = value + ref[i]
         return value
 
-    w1[x] = term[rows(x * 32, 32), :]
-    for d in (2, 1, 3):
-        share(0, term.at[rows((x + d) % 4 * 32, 32)], w1.at[x], at(x + d, y)).start()
+    half_rows = rows(core * 64, 64)
+    share(0, term.at[rows((1 - core) * 64, 64)], w1, partner).start()
 
     loads[4].wait()
     loads[5].wait()
@@ -183,11 +182,12 @@
                 gather_copy(h, r, first_recv.at[h * 6 + e * 3 + d - 1], toward(e, 0, d)).wait_recv()
                 second(h, e, r)
 
-    plain(w1.at[pl.ds(0, 3)], w_recv.at[0]).wait()
-    w1s[...] = added(w1, 4)
-    w2[y] = w1s[rows(y * 8, 8), :]
-    for d in (2, 1, 3):
-        share(1, w1s.at[rows((y + d) % 4 * 8, 8)], w2.at[y], at(x, y + d)).start()
+    share(0, w1, w1, partner).wait_recv()
+    w1s[...] = term[half_rows, :] + w1[...]
+    w2[z] = w1s[rows(z * 8, 8), :]
+    pl.semaphore_wait(near_sem, 2)
+    for d in (4, 3, 5, 2, 6, 1, 7):
+        share(1, w1s.at[rows((z + d) % 8 * 8, 8)], w2.at[z], up(d)).start()
 
     to_scalar.wait()
     for load in tile_loads:
@@ -276,45 +276,39 @@
         return result
 
     gathered(0)
-    plain(w2.at[pl.ds(0, 3)], w_recv.at[1]).wait()
-    w3[core] = added(w2, 4)
-    share(2, w3.at[core], w3.at[core], partner).start()
-
     products(0)
     scatter_swap(0)
-
-    share(2, w3.at[core], w3.at[1 - core], partner).wait_recv()
-    w4[z] = w3[0] + w3[1]
-    pl.semaphore_wait(near_sem, 2)
-    for d in (4, 3, 5, 2, 6, 1, 7):
-        share(3, w4.at[z], w4.at[z], up(d)).start()
+    plain(w2.at[pl.ds(0, 7)], w_recv.at[1]).wait()
+    w3[x] = added(w2, 8)
+    for d in (2, 1, 3):
+        share(2, w3.at[x], w3.at[x], at(x + d, y)).start()
     scatter_near(0)
-
     gathered(1)
     products(1)
     scatter_swap(1)
+    plain(w3.at[pl.ds(0, 3)], w_recv.at[2]).wait()
+    w4[y] = added(w3, 4)
+    for d in (2, 1, 3):
+        share(3, w4.at[y], w4.at[y], at(x, y + d)).start()
+    scatter_near(1)
     scatter_far(0)
-    scatter_near(1)
-
-    plain(w4.at[pl.ds(0, 7)], w_recv.at[3]).wait()
-    mine_rows = rows(x * 32 + y * 8, 8)
-    weight_grad[mine_rows, :] = added(w4, 8)
-    for d in (2, 1, 3):
-        share(4, weight_grad.at[mine_rows], weight_grad.at[mine_rows], at(x, y + d)).start()
+    plain(w4.at[pl.ds(0, 3)], w_recv.at[3]).wait()
+    mine_rows = rows(core * 64 + z * 8, 8)
+    weight_grad[mine_rows, :] = added(w4, 4)
+    for d in (4, 3, 5, 2, 6, 1, 7):
+        share(4, weight_grad.at[mine_rows], weight_grad.at[mine_rows], up(d)).start()
+    scatter_far(1)
+
     first_half = scattered(0)
-    scatter_far(1)
-    plain(weight_grad.at[pl.ds(0, 24)], w_recv.at[4]).wait()
-    line_rows = rows(x * 32, 32)
-    for d in (2, 1, 3):
-        share(5, weight_grad.at[line_rows], weight_grad.at[line_rows], at(x + d, y)).start()
-
+    plain(weight_grad.at[pl.ds(0, 56)], w_recv.at[4]).wait()
+    share(5, weight_grad.at[half_rows], weight_grad.at[half_rows], partner).start()
     second_half = scattered(1)
     for e in range(2):
         whole = jnp.concatenate([first_half[e], second_half[e]], axis=0)
         input_grad[e * TILE : (e + 1) * TILE, :] = whole.T.astype(BF16)
 
-    plain(weight_grad.at[pl.ds(0, 96)], w_recv.at[5]).wait()
-    for i, size in enumerate((96, 24, 8, 56, 24, 96)):
+    plain(weight_grad.at[pl.ds(0, 64)], w_recv.at[5]).wait()
+    for i, size in enumerate((64, 56, 24, 24, 56, 64)):
         plain(term.at[pl.ds(0, size)], w_send.at[i]).wait()
     for h in range(2):
         plain(aggs[h].at[pl.ds(0, 30)], gather_send.at[h]).wait()
@@ -324,10 +318,21 @@
             scatter_copy(h, r).wait_send()
 
 
+def write_out(input_grad, weight_grad, input_out, weight_out, sems):
+    copies = [
+        pltpu.make_async_copy(input_grad, input_out, sems.at[0]),
+        pltpu.make_async_copy(weight_grad, weight_out, sems.at[1]),
+    ]
+    for copy in copies:
+        copy.start()
+    for copy in copies:
+        copy.wait()
+
+
 def local(out_grad, relu_mask, saved_agg, weight, tile_values, tile_coords, tile_count):
     nodes = out_grad.shape[0]
     vmem, dma = pltpu.VMEM, pltpu.SemaphoreType.DMA
-    return pl.pallas_call(
+    results = pl.pallas_call(
         kernel,
         out_shape=(
             pltpu.VMEM((nodes, TILE), BF16),
@@ -355,11 +360,11 @@
             vmem((2, 7, 2, HALF, TILE), BF16),
             vmem((2, 3, 2, HALF, TILE), F32),
             vmem((TILE, TILE), F32),
-            vmem((4, 32, TILE), F32),
-            vmem((32, TILE), F32),
+            vmem((64, TILE), F32),
+            vmem((64, TILE), F32),
+            vmem((8, 8, TILE), F32),
             vmem((4, 8, TILE), F32),
-            vmem((2, 8, TILE), F32),
-            vmem((8, 8, TILE), F32),
+            vmem((4, 8, TILE), F32),
             dma((7,)),
             dma((CHUNKS,)),
             dma((12,)),
@@ -380,6 +385,13 @@
         pltpu.with_memory_space_constraint(array, pltpu.HBM)
         for array in (out_grad, relu_mask, saved_agg, weight, tile_values, tile_coords[0, 0].T)
     ], tile_count)
+    return pl.pallas_call(
+        write_out,
+        out_shape=(pltpu.HBM((nodes, TILE), BF16), pltpu.HBM((TILE, TILE), F32)),
+        in_specs=[pl.BlockSpec(memory_space=pltpu.VMEM)] * 2,
+        out_specs=[pl.BlockSpec(memory_space=pltpu.HBM)] * 2,
+        scratch_shapes=[dma((2,))],
+    )(*[pltpu.with_memory_space_constraint(result, pltpu.VMEM) for result in results])
 
 
 def solution(mesh):

time: 38.8 us -> 35.4 us (0.912)
  Pallas kernels: 36.2 us -> 34 us
  local copies, waits for them, and re-layouts: 1.26 us -> 0 us
    pallas_call x1, Pallas kernels: 36.2 us -> 33.3 us  [local(): pl.pallas_call(kernel, out_shape=(pltpu.VMEM((nodes, TILE), BF16), pltpu....]
    unnamed x2 -> x0, local copies, waits for them, and re-layouts: 1.26 us -> none
    pallas_call x0 -> x1, Pallas kernels: none -> 0.67 us  [local(): pl.pallas_call(write_out, out_shape=(pltpu.HBM((nodes, TILE), BF16), pltp...]
where the time goes in v3:
time: 35.4 us; the launch traced here: 35.3 us
  Pallas kernels  34 us (96%)
  between operations  1.29 us (4%)
    pallas_call x1, Pallas kernels, local(): pl.pallas_call(kernel, out_shape=(pltpu.VMEM((nodes, TILE), BF16), pltpu....  33.3 us

profile of v3, /device:TPU:1, one launch (start us, length us, event | category | flops | bytes accessed | tf_op | source)
XLA Modules:
  0.0 35.3 jit_solution(17757022095027426849)
XLA Ops:
  1.3 33.3 %shard_map.86 = (bf16[256,128]{1,0:T(8,128)(2,1)S(1)}, f32[128,128]{1,0:T(8,128)S(1)}) custom-call(bf16[256,128]{1,0:T(8,128)(2,1)} %out_grad.1, bf16[256,128]{1,0:T(8,128)(2,1)} %relu_mask.1, bf16[256,128]{1,0:T(8,128)(2,1)} %saved_agg.1, bf16[128,128]{1,0:T(8,128)(2,1)} %weight.1, bf16[1,1,320,128,128]{4,3,2,1,0:T(8,128)(2,1)} %tile_values.1, ...), custom_call_target="tpu_custom_call" | custom-call | tf_op jit(solution)/shard_map/pallas_call | solution.py:335
  34.6 0.7 %shard_map.87 = (bf16[256,128]{1,0:T(8,128)(2,1)}, f32[128,128]{1,0:T(8,128)}) custom-call(bf16[256,128]{1,0:T(8,128)(2,1)S(1)} %get-tuple-element.4.input_grad, f32[128,128]{1,0:T(8,128)S(1)} %get-tuple-element.5.weight_grad), custom_call_target="tpu_custom_call" | custom-call | tf_op jit(solution)/shard_map/pallas_call | solution.py:388

commit v4 on v3

--- a/solution.py
+++ b/solution.py
@@ -60,7 +60,7 @@
 def kernel(
     out_grad, relu_mask, saved_agg, weight, tile_values, coords, count, input_grad, weight_grad,
     og, rm, sa, wt, tiles, xy, ct, meta_v, meta,
-    agg0, agg1, run0, run1, xsend, xrecv, zsend, zrecv, own, term, w1, w1s, w2, w3, w4,
+    agg0, agg1, run0, run1, xsend, xrecv, zsend, zrecv, own, term, w1, w1s, w2, w3,
     load_sem, tile_sem, first_recv, second_recv, gather_send,
     xs_sem, xr_sem, zs_sem, zr_sem, w_send, w_recv, near_sem,
 ):
@@ -175,19 +175,19 @@
     to_scalar = pltpu.make_async_copy(meta_v, meta, load_sem.at[6])
     to_scalar.start()
 
+    share(0, w1, w1, partner).wait_recv()
+    w1s[...] = term[half_rows, :] + w1[...]
+    w2[z] = w1s[rows(z * 8, 8), :]
+    pl.semaphore_wait(near_sem, 2)
+    for d in (4, 3, 5, 2, 6, 1, 7):
+        share(1, w1s.at[rows((z + d) % 8 * 8, 8)], w2.at[z], up(d)).start()
+
     for h in range(2):
         for d in (1, 3, 2):
             for e in range(2):
                 r = piece(e, d)
                 gather_copy(h, r, first_recv.at[h * 6 + e * 3 + d - 1], toward(e, 0, d)).wait_recv()
                 second(h, e, r)
-
-    share(0, w1, w1, partner).wait_recv()
-    w1s[...] = term[half_rows, :] + w1[...]
-    w2[z] = w1s[rows(z * 8, 8), :]
-    pl.semaphore_wait(near_sem, 2)
-    for d in (4, 3, 5, 2, 6, 1, 7):
-        share(1, w1s.at[rows((z + d) % 8 * 8, 8)], w2.at[z], up(d)).start()
 
     to_scalar.wait()
     for load in tile_loads:
@@ -276,27 +276,23 @@
         return result
 
     gathered(0)
+    plain(w2.at[pl.ds(0, 7)], w_recv.at[1]).wait()
+    w3[col] = added(w2, 8)
+    for a, b in ((2, 2), (1, 2), (3, 2), (2, 1), (2, 3), (0, 2), (2, 0), (1, 1), (1, 3), (3, 1), (3, 3), (0, 1), (0, 3), (1, 0), (3, 0)):
+        share(2, w3.at[col], w3.at[col], at(x + a, y + b)).start()
     products(0)
     scatter_swap(0)
-    plain(w2.at[pl.ds(0, 7)], w_recv.at[1]).wait()
-    w3[x] = added(w2, 8)
-    for d in (2, 1, 3):
-        share(2, w3.at[x], w3.at[x], at(x + d, y)).start()
     scatter_near(0)
     gathered(1)
     products(1)
     scatter_swap(1)
-    plain(w3.at[pl.ds(0, 3)], w_recv.at[2]).wait()
-    w4[y] = added(w3, 4)
-    for d in (2, 1, 3):
-        share(3, w4.at[y], w4.at[y], at(x, y + d)).start()
+    plain(w3.at[pl.ds(0, 15)], w_recv.at[2]).wait()
+    mine_rows = rows(core * 64 + z * 8, 8)
+    weight_grad[mine_rows, :] = added(w3, 16)
+    for d in (4, 3, 5, 2, 6, 1, 7):
+        share(4, weight_grad.at[mine_rows], weight_grad.at[mine_rows], up(d)).start()
     scatter_near(1)
     scatter_far(0)
-    plain(w4.at[pl.ds(0, 3)], w_recv.at[3]).wait()
-    mine_rows = rows(core * 64 + z * 8, 8)
-    weight_grad[mine_rows, :] = added(w4, 4)
-    for d in (4, 3, 5, 2, 6, 1, 7):
-        share(4, weight_grad.at[mine_rows], weight_grad.at[mine_rows], up(d)).start()
     scatter_far(1)
 
     first_half = scattered(0)
@@ -308,7 +304,7 @@
         input_grad[e * TILE : (e + 1) * TILE, :] = whole.T.astype(BF16)
 
     plain(weight_grad.at[pl.ds(0, 64)], w_recv.at[5]).wait()
-    for i, size in enumerate((64, 56, 24, 24, 56, 64)):
+    for i, size in ((0, 64), (1, 56), (2, 120), (4, 56), (5, 64)):
         plain(term.at[pl.ds(0, size)], w_send.at[i]).wait()
     for h in range(2):
         plain(aggs[h].at[pl.ds(0, 30)], gather_send.at[h]).wait()
@@ -363,8 +359,7 @@
             vmem((64, TILE), F32),
             vmem((64, TILE), F32),
             vmem((8, 8, TILE), F32),
-            vmem((4, 8, TILE), F32),
-            vmem((4, 8, TILE), F32),
+            vmem((16, 8, TILE), F32),
             dma((7,)),
             dma((CHUNKS,)),
             dma((12,)),

time: 35.4 us -> 34.9 us (0.986)
  Pallas kernels: 34 us -> 33.5 us
    pallas_call x1, Pallas kernels: 33.3 us -> 32.8 us  [local(): pl.pallas_call(kernel, out_shape=(pltpu.VMEM((nodes, TILE), BF16), pltpu....]
where the time goes in v4:
time: 34.9 us; the launch traced here: 34.8 us
  Pallas kernels  33.5 us (96%)
  between operations  1.29 us (4%)
    pallas_call x1, Pallas kernels, local(): pl.pallas_call(kernel, out_shape=(pltpu.VMEM((nodes, TILE), BF16), pltpu....  32.8 us

profile of v4, /device:TPU:1, one launch (start us, length us, event | category | flops | bytes accessed | tf_op | source)
XLA Modules:
  0.0 34.8 jit_solution(11556306630910728940)
XLA Ops:
  1.3 32.8 %shard_map.86 = (bf16[256,128]{1,0:T(8,128)(2,1)S(1)}, f32[128,128]{1,0:T(8,128)S(1)}) custom-call(bf16[256,128]{1,0:T(8,128)(2,1)} %out_grad.1, bf16[256,128]{1,0:T(8,128)(2,1)} %relu_mask.1, bf16[256,128]{1,0:T(8,128)(2,1)} %saved_agg.1, bf16[128,128]{1,0:T(8,128)(2,1)} %weight.1, bf16[1,1,320,128,128]{4,3,2,1,0:T(8,128)(2,1)} %tile_values.1, ...), custom_call_target="tpu_custom_call" | custom-call | tf_op jit(solution)/shard_map/pallas_call | solution.py:331
  34.1 0.7 %shard_map.87 = (bf16[256,128]{1,0:T(8,128)(2,1)}, f32[128,128]{1,0:T(8,128)}) custom-call(bf16[256,128]{1,0:T(8,128)(2,1)S(1)} %get-tuple-element.4.input_grad, f32[128,128]{1,0:T(8,128)S(1)} %get-tuple-element.5.weight_grad), custom_call_target="tpu_custom_call" | custom-call | tf_op jit(solution)/shard_map/pallas_call | solution.py:383

commit v5 on v4

--- a/solution.py
+++ b/solution.py
@@ -114,57 +114,6 @@
         for e in range(2):
             aggs[h][2 * col + e] = mine[h * HALF : (h + 1) * HALF, e * TILE : (e + 1) * TILE]
 
-    pl.semaphore_wait(barrier, len(peers))
-    for d in (2, 6):
-        pl.semaphore_signal(near_sem, inc=1, device_id=up(d), device_id_type=MESH)
-
-    def toward(e, phase, d):
-        return at(x + d, y) if (e + phase) % 2 == 0 else at(x, y + d)
-
-    def piece(e, d):
-        a, b = ((x - d) % 4, y) if e == 0 else (x, (y - d) % 4)
-        return 2 * (a * 4 + b) + e
-
-    def gather_copy(h, r, recv, target):
-        block = aggs[h].at[r]
-        return pltpu.make_async_remote_copy(
-            src_ref=block, dst_ref=block, send_sem=gather_send.at[h], recv_sem=recv, device_id=target, device_id_type=MESH
-        )
-
-    def second(h, e, r):
-        for d in (2, 1, 3):
-            gather_copy(h, r, second_recv.at[h], toward(e, 1, d)).start()
-
-    for h in range(2):
-        for e in range(2):
-            for d in (2, 1, 3):
-                gather_copy(h, 2 * col + e, first_recv.at[h * 6 + e * 3 + d - 1], toward(e, 0, d)).start()
-        for e in range(2):
-            second(h, e, 2 * col + e)
-
-    loads[3].wait()
-    term[...] = lax.dot_general(sa[...], pre, (((0,), (0,)), ((), ())), preferred_element_type=F32)
-
-    def rows(start, size):
-        return pl.ds(pl.multiple_of(start, 8), size)
-
-    def share(i, src, dst, target):
-        return pltpu.make_async_remote_copy(
-            src_ref=src, dst_ref=dst, send_sem=w_send.at[i], recv_sem=w_recv.at[i], device_id=target, device_id_type=MESH
-        )
-
-    def plain(ref, sem):
-        return pltpu.make_async_copy(ref, ref, sem)
-
-    def added(ref, n):
-        value = ref[0]
-        for i in range(1, n):
-            value = value + ref[i]
-        return value
-
-    half_rows = rows(core * 64, 64)
-    share(0, term.at[rows((1 - core) * 64, 64)], w1, partner).start()
-
     loads[4].wait()
     loads[5].wait()
     packed, keep, last = order_slots(xy[...], ct[...])
@@ -175,6 +124,57 @@
     to_scalar = pltpu.make_async_copy(meta_v, meta, load_sem.at[6])
     to_scalar.start()
 
+    pl.semaphore_wait(barrier, len(peers))
+    for d in (2, 6):
+        pl.semaphore_signal(near_sem, inc=1, device_id=up(d), device_id_type=MESH)
+
+    def toward(e, phase, d):
+        return at(x + d, y) if (e + phase) % 2 == 0 else at(x, y + d)
+
+    def piece(e, d):
+        a, b = ((x - d) % 4, y) if e == 0 else (x, (y - d) % 4)
+        return 2 * (a * 4 + b) + e
+
+    def gather_copy(h, r, recv, target):
+        block = aggs[h].at[r]
+        return pltpu.make_async_remote_copy(
+            src_ref=block, dst_ref=block, send_sem=gather_send.at[h], recv_sem=recv, device_id=target, device_id_type=MESH
+        )
+
+    def second(h, e, r):
+        for d in (2, 1, 3):
+            gather_copy(h, r, second_recv.at[h], toward(e, 1, d)).start()
+
+    for h in range(2):
+        for e in range(2):
+            for d in (2, 1, 3):
+                gather_copy(h, 2 * col + e, first_recv.at[h * 6 + e * 3 + d - 1], toward(e, 0, d)).start()
+        for e in range(2):
+            second(h, e, 2 * col + e)
+
+    loads[3].wait()
+    term[...] = lax.dot_general(sa[...], pre, (((0,), (0,)), ((), ())), preferred_element_type=F32)
+
+    def rows(start, size):
+        return pl.ds(pl.multiple_of(start, 8), size)
+
+    def share(i, src, dst, target):
+        return pltpu.make_async_remote_copy(
+            src_ref=src, dst_ref=dst, send_sem=w_send.at[i], recv_sem=w_recv.at[i], device_id=target, device_id_type=MESH
+        )
+
+    def plain(ref, sem):
+        return pltpu.make_async_copy(ref, ref, sem)
+
+    def added(ref, n):
+        value = ref[0]
+        for i in range(1, n):
+            value = value + ref[i]
+        return value
+
+    half_rows = rows(core * 64, 64)
+    share(0, term.at[rows((1 - core) * 64, 64)], w1, partner).start()
+
     share(0, w1, w1, partner).wait_recv()
     w1s[...] = term[half_rows, :] + w1[...]
     w2[z] = w1s[rows(z * 8, 8), :]
@@ -241,20 +241,25 @@
         slot = (2 - turn * r + 8) % 8
         return column(h, (z - turn * r + 8) % 8, core, e) + xrecv[h, slot, e].astype(F32)
 
-    def scatter_near(h):
-        swap(h, True).wait_recv()
-        for r in roles[:5]:
-            if r == 1:
-                swap(h, False).wait_recv()
+    def send_roles(h, some):
+        for r in some:
             for e in range(2):
                 zsend[h, roles.index(r), e] = pair_sum(h, r, e).astype(BF16)
             scatter_copy(h, r).start()
+
+    def scatter_first(h):
+        swap(h, True).wait_recv()
+        send_roles(h, roles[:3])
+
+    def scatter_near(h):
+        swap(h, False).wait_recv()
+        send_roles(h, roles[3:5])
         for i, r in enumerate((2, -2, 0)):
             for e in range(2):
                 own[h, i, e] = pair_sum(h, r, e)
 
     def scatter_far(h):
-        for r, sources in ((2, (4, 3)), (-2, (-3,))):
+        for r, sources in ((-2, (-3,)), (2, (4, 3))):
             for q in sources:
                 scatter_copy(h, q).wait_recv()
             for e in range(2):
@@ -282,6 +287,7 @@
         share(2, w3.at[col], w3.at[col], at(x + a, y + b)).start()
     products(0)
     scatter_swap(0)
+    scatter_first(0)
     scatter_near(0)
     gathered(1)
     products(1)
@@ -291,8 +297,9 @@
     weight_grad[mine_rows, :] = added(w3, 16)
     for d in (4, 3, 5, 2, 6, 1, 7):
         share(4, weight_grad.at[mine_rows], weight_grad.at[mine_rows], up(d)).start()
+    scatter_first(1)
+    scatter_far(0)
     scatter_near(1)
-    scatter_far(0)
     scatter_far(1)
 
     first_half = scattered(0)

time: 34.9 us -> 34.1 us (0.977)
  Pallas kernels: 33.5 us -> 32.7 us
    pallas_call x1, Pallas kernels: 32.8 us -> 32 us  [local(): pl.pallas_call(kernel, out_shape=(pltpu.VMEM((nodes, TILE), BF16), pltpu....]
where the time goes in v5:
time: 34.1 us; the launch traced here: 34 us
  Pallas kernels  32.7 us (96%)
  between operations  1.29 us (4%)
    pallas_call x1, Pallas kernels, local(): pl.pallas_call(kernel, out_shape=(pltpu.VMEM((nodes, TILE), BF16), pltpu....  32 us

profile of v5, /device:TPU:1, one launch (start us, length us, event | category | flops | bytes accessed | tf_op | source)
XLA Modules:
  0.0 34.0 jit_solution(13201820830435900695)
XLA Ops:
  1.3 32.0 %shard_map.86 = (bf16[256,128]{1,0:T(8,128)(2,1)S(1)}, f32[128,128]{1,0:T(8,128)S(1)}) custom-call(bf16[256,128]{1,0:T(8,128)(2,1)} %out_grad.1, bf16[256,128]{1,0:T(8,128)(2,1)} %relu_mask.1, bf16[256,128]{1,0:T(8,128)(2,1)} %saved_agg.1, bf16[128,128]{1,0:T(8,128)(2,1)} %weight.1, bf16[1,1,320,128,128]{4,3,2,1,0:T(8,128)(2,1)} %tile_values.1, ...), custom_call_target="tpu_custom_call" | custom-call | tf_op jit(solution)/shard_map/pallas_call | solution.py:338
  33.3 0.7 %shard_map.87 = (bf16[256,128]{1,0:T(8,128)(2,1)}, f32[128,128]{1,0:T(8,128)}) custom-call(bf16[256,128]{1,0:T(8,128)(2,1)S(1)} %get-tuple-element.4.input_grad, f32[128,128]{1,0:T(8,128)S(1)} %get-tuple-element.5.weight_grad), custom_call_target="tpu_custom_call" | custom-call | tf_op jit(solution)/shard_map/pallas_call | solution.py:390

commit v6 on v5

--- a/solution.py
+++ b/solution.py
@@ -302,13 +302,14 @@
     scatter_near(1)
     scatter_far(1)
 
-    first_half = scattered(0)
+    def finish(h):
+        for e, value in enumerate(scattered(h)):
+            input_grad[e * TILE : (e + 1) * TILE, h * HALF : (h + 1) * HALF] = value.T.astype(BF16)
+
+    finish(0)
     plain(weight_grad.at[pl.ds(0, 56)], w_recv.at[4]).wait()
     share(5, weight_grad.at[half_rows], weight_grad.at[half_rows], partner).start()
-    second_half = scattered(1)
-    for e in range(2):
-        whole = jnp.concatenate([first_half[e], second_half[e]], axis=0)
-        input_grad[e * TILE : (e + 1) * TILE, :] = whole.T.astype(BF16)
+    finish(1)
 
     plain(weight_grad.at[pl.ds(0, 64)], w_recv.at[5]).wait()
     for i, size in ((0, 64), (1, 56), (2, 120), (4, 56), (5, 64)):

time: 34.1 us -> 34.2 us (level)
  no operation moved by 1% of the time
where the time goes in v6:
time: 34.2 us; the launch traced here: 34.1 us
  Pallas kernels  32.8 us (96%)
  between operations  1.29 us (4%)
    pallas_call x1, Pallas kernels, local(): pl.pallas_call(kernel, out_shape=(pltpu.VMEM((nodes, TILE), BF16), pltpu....  32.1 us

profile of v6, /device:TPU:1, one launch (start us, length us, event | category | flops | bytes accessed | tf_op | source)
XLA Modules:
  0.0 34.1 jit_solution(8711499961880154681)
XLA Ops:
  1.3 32.1 %shard_map.86 = (bf16[256,128]{1,0:T(8,128)(2,1)S(1)}, f32[128,128]{1,0:T(8,128)S(1)}) custom-call(bf16[256,128]{1,0:T(8,128)(2,1)} %out_grad.1, bf16[256,128]{1,0:T(8,128)(2,1)} %relu_mask.1, bf16[256,128]{1,0:T(8,128)(2,1)} %saved_agg.1, bf16[128,128]{1,0:T(8,128)(2,1)} %weight.1, bf16[1,1,320,128,128]{4,3,2,1,0:T(8,128)(2,1)} %tile_values.1, ...), custom_call_target="tpu_custom_call" | custom-call | tf_op jit(solution)/shard_map/pallas_call | solution.py:339
  33.4 0.7 %shard_map.87 = (bf16[256,128]{1,0:T(8,128)(2,1)}, f32[128,128]{1,0:T(8,128)}) custom-call(bf16[256,128]{1,0:T(8,128)(2,1)S(1)} %get-tuple-element.4.input_grad, f32[128,128]{1,0:T(8,128)S(1)} %get-tuple-element.5.weight_grad), custom_call_target="tpu_custom_call" | custom-call | tf_op jit(solution)/shard_map/pallas_call | solution.py:391
